TPU v7x, 32 devices: a whole 2x2x4 slice. The times are simulated.
32 devices in a mesh: row: 4 (over y, core), src: 8 (over z, x).
Axes of the slice: x: 2, y: 2, z: 4, core: 2. Of those that a mesh axis runs over, the one named last changes fastest.
Arguments:
- front_panel: float32 [3, 256, 8192], P(None, None, ('row', 'src')), may hold values from -0.0625 to 0.0625
- solved_prev: float32 [8192, 2048], P('row', 'src'), may hold values from -6 to 6
- right_side: float32 [768, 2048], P(None, 'src'), may hold values from -6 to 6
- front_window: float32 [768, 768], replicated, may hold values from -0.21875 to 0.21875
- inv_diag: float32 [3, 256, 256], replicated, may hold values from -0.375 to 0.375
- owner_map: int32 [3], replicated, may hold values from 0 to 3, as said below
Outputs:
- stored: float32 [1024, 2048], P('row', 'src')
Inputs may be any that keep to these rules, and one draw needn't show every extreme that they name: `owner_map`: the blocks' owners are distinct row groups.
All inputs are finite; a program needn't handle non-finite values.
Results may differ from a plain program's by a relative error of at most 0.0001.
Values sent between devices are 32-bit elements; how exact they have to be, the bound alone decides.
A program may use at most 64 MiB of HBM per device.

v0:
```python
import jax
import jax.numpy as jnp
from jax import lax
from jax.sharding import PartitionSpec as P


def body(front_panel, solved_prev, right_side, front_window, inv_diag, owner_map):
    highest = lax.Precision.HIGHEST
    nblk = front_panel.shape[0]
    block = front_panel.shape[1]
    width = solved_prev.shape[1]
    here = lax.axis_index("row")
    panel_rows = lax.all_gather(front_panel, "src", axis=2, tiled=True)
    local = jnp.einsum(
        "kbn,ns->kbs",
        panel_rows,
        solved_prev,
        precision=highest,
        preferred_element_type=jnp.float32,
    )
    partials = lax.psum(local, "row")
    stored = jnp.zeros((block, width), jnp.float32)
    solutions = []
    for k in range(nblk):
        partial_value = partials[k]
        rhs = right_side[k * block : (k + 1) * block] - partial_value
        if k > 0:
            earlier = jnp.concatenate(solutions, axis=0)
            rhs = rhs - jnp.dot(
                front_window[k * block : (k + 1) * block, : k * block],
                earlier,
                precision=highest,
                preferred_element_type=jnp.float32,
            )
        mine = here == owner_map[k]
        solution = jnp.dot(inv_diag[k], rhs, precision=highest, preferred_element_type=jnp.float32)
        solutions.append(solution)
        stored = stored + jnp.where(mine, solution, jnp.zeros_like(solution))
    return stored


def solution(mesh):
    in_specs = (P(None, None, ("row", "src")), P("row", "src"), P(None, "src"), P(), P(), P())
    out_specs = P("row", "src")
    return jax.shard_map(body, mesh=mesh, in_specs=in_specs, out_specs=out_specs, check_vma=False)
```

profile of v0, /device:TPU:0, one launch (start us, length us, event | category | flops | bytes accessed | tf_op | source)
XLA Modules:
  0.0 168.3 jit_solution(15583555766104265362)
XLA Ops:
  6.5 0.0 copy-start
  6.5 0.0 all-gather.2.cloned.1.call-start
  6.5 0.7 all-gather.2.cloned.1.call-update
  7.3 0.0 copy-start.2
  7.3 0.0 copy-start.1
  7.3 0.0 all-reduce.2.cloned.1.call-start
  7.3 104.7 %all-gather.2.cloned.1.call-done = f32[3,256,2048]{2,1,0:T(8,128)} async-done(((f32[3,256,256]{2,1,0:T(8,128)}), f32[3,256,2048]{2,1,0:T(8,128)}) %all-gather.2.cloned.1.call-update) | async-done | bytes 6291472 | tf_op jit(solution)/shard_map/all_gather | solution.py:13
  112.1 0.0 copy-done
  112.1 8.0 %fusion = f32[3,256,256]{2,1,0:T(8,128)} fusion(f32[3,256,2048]{2,1,0:T(8,128)} %all-gather.2.cloned.1.call-done, f32[2048,256]{1,0:T(8,128)S(1)} %copy-done), kind=kOutput, calls=%fused_computation | convolution fusion | flops 4831838208 | bytes 9175040 | tf_op jit(solution)/shard_map/kbn,ns->kbs/dot_general | solution.py:14
  120.1 0.0 all-reduce.2.cloned.1.call-update
  120.1 0.0 copy-done.2
  120.1 0.7 fusion.24
  122.7 30.4 %all-reduce.2.cloned.1.call-done = f32[3,256,256]{2,1,0:T(8,128)} async-done(((f32[3,256,256]{2,1,0:T(8,128)}), f32[3,256,256]{2,1,0:T(8,128)}) %all-reduce.2.cloned.1.call-update) | async-done | bytes 786448 | tf_op jit(solution)/shard_map/psum | solution.py:21
  153.1 0.0 copy-done.1
  153.1 1.4 fusion.13
  154.5 1.4 fusion.4
  156.0 1.4 convolution_bitcast_fusion.1
  157.3 0.1 copy.7
  157.5 0.1 copy.9
  157.6 1.8 %fusion.5 = f32[256,256]{1,0:T(8,128)S(1)} fusion(f32[256,256]{1,0:T(8,128)S(1)} %convolution_bitcast_fusion.1, f32[256,256]{1,0:T(8,128)S(1)} %bitcast.52, f32[768,768]{1,0:T(8,128)} %param.9, f32[3,256,256]{2,1,0:T(8,128)} %all-reduce.2.cloned.1.call-done, f32[768,256]{1,0:T(8,128)} %param.8), kind=kOutput, calls=%fused_computation.9 | convolution fusion | flops 402915328 | bytes 1835008 | tf_op jit(solution)/shard_map/dot_general | solution.py:29
  159.4 2.1 %fusion.3 = f32[256,256]{1,0:T(8,128)} fusion(f32[256,256]{1,0:T(8,128)S(1)} %fusion.5, f32[3,256,256]{2,1,0:T(8,128)} %param.10, f32[256,256]{1,0:T(8,128)S(1)} %copy.9, f32[256,256]{1,0:T(8,128)S(1)} %convolution_bitcast_fusion.1, pred[]{:T(512)S(6)} %eq.11, pred[]{:T(512)S(6)} %eq.10), kind=kOutput, calls=%fused_computation.4 | convolution fusion | flops 201588736 | bytes 1310722 | tf_op jit(solution)/shard_map/dot_general | solution.py:36
  (1 shorter events, 0.0 us)
Async XLA Ops:
  6.5 105.5 %copy-start = (f32[2048,256]{1,0:T(8,128)S(1)}, f32[2048,256]{1,0:T(8,128)}, u32[]{:S(2)}) copy-start(f32[2048,256]{1,0:T(8,128)} %param.7) | copy-start | bytes 6291460
  6.5 105.5 %all-gather.2.cloned.1.call-start = ((), (), s32[]{:S(2)}) async-start(), calls=%async_computation | async-start | bytes 7077888 | tf_op jit(solution)/shard_map/all_gather | solution.py:13
  7.3 112.9 %copy-start.2 = (s32[3]{0:T(128)S(1)}, s32[3]{0:T(128)}, u32[]{:S(2)}) copy-start(s32[3]{0:T(128)} %param.11) | copy-start | bytes 40
  7.3 145.8 %copy-start.1 = (f32[768,256]{1,0:T(8,128)S(1)}, f32[768,256]{1,0:T(8,128)}, u32[]{:S(2)}) copy-start(f32[768,256]{1,0:T(8,128)} %param.8) | copy-start | bytes 2359300
  7.3 145.8 %all-reduce.2.cloned.1.call-start = ((), (), s32[]{:S(2)}) async-start(), calls=%async_computation.1 | async-start | bytes 1572864 | tf_op jit(solution)/shard_map/psum | solution.py:21
Sparse Core Ops, SparseCore 0:
  9.4 102.6 all-gather.1
  120.2 32.8 all-reduce.1
where the time goes:
time: 169 us; the launch traced here: 168 us
  waiting for transfers between devices  136 us (80%)
  matrix products  16.1 us (10%)
  between operations  15.4 us (9%)
    all_gather x1, waiting for transfers between devices, body(): panel_rows = lax.all_gather(front_panel, 'src', axis=2, tiled=True)  105 us
    psum x1, waiting for transfers between devices, body(): partials = lax.psum(local, 'row')  30.4 us
    dot_general x1, matrix products, body(): jnp.einsum('kbn,ns->kbs', panel_rows, solved_prev, precision=highest, pre...  8.01 us
    dot_general x3, matrix products, body(): jnp.dot(inv_diag[k], rhs, precision=highest, preferred_element_type=jnp.f...  4.84 us
  transfers between devices with their start and end apart: 2, of which 2 were waited for; matrix products, arithmetic and copies ran while one was open for 0% of the time, Pallas kernels for 0%

commit v1 on v0

--- a/solution.py
+++ b/solution.py
@@ -1,10 +1,18 @@
+import functools
+
 import jax
 import jax.numpy as jnp
 from jax import lax
+from jax.experimental import pallas as pl
+from jax.experimental.pallas import tpu as pltpu
 from jax.sharding import PartitionSpec as P
 
-
-def body(front_panel, solved_prev, right_side, front_window, inv_diag, owner_map):
+F32 = jnp.float32
+BF16 = jnp.bfloat16
+MESH = pl.DeviceIdType.MESH
+
+
+def general_body(front_panel, solved_prev, right_side, front_window, inv_diag, owner_map):
     highest = lax.Precision.HIGHEST
     nblk = front_panel.shape[0]
     block = front_panel.shape[1]
@@ -22,8 +30,7 @@
     stored = jnp.zeros((block, width), jnp.float32)
     solutions = []
     for k in range(nblk):
-        partial_value = partials[k]
-        rhs = right_side[k * block : (k + 1) * block] - partial_value
+        rhs = right_side[k * block : (k + 1) * block] - partials[k]
         if k > 0:
             earlier = jnp.concatenate(solutions, axis=0)
             rhs = rhs - jnp.dot(
@@ -39,7 +46,246 @@
     return stored
 
 
+def split(v):
+    hi = v.astype(BF16)
+    return hi, (v - hi.astype(F32)).astype(BF16)
+
+
+def dot(a, b):
+    return jnp.dot(a, b, preferred_element_type=F32)
+
+
+def dot3(a, b):
+    (ah, al), (bh, bl) = split(a), split(b)
+    return dot(ah, bh) + (dot(ah, bl) + dot(al, bh))
+
+
+def kernel(
+    nz, n_row, owner, fp, sp, rs, win, inv, out,
+    ga, rb, bh, bl, ah, al, acc, rc, sx, rx, ty, ry, fs, fr,
+    zr_send, zl_send, z_recv, b_send, b_recv, c_send, c_recv, x_send, x_recv, y_send, y_recv, f_sem,
+):
+    nblk, block, kc = fp.shape
+    width = sp.shape[1]
+    half = width // 2
+    row, src = lax.axis_index("row"), lax.axis_index("src")
+    z, x = src // 2, lax.rem(src, 2)
+    core = lax.rem(row, 2)
+    sib = row + 1 - 2 * core
+    yp = lax.rem(row + 2, n_row)
+    xp = src + 1 - 2 * x
+    has_l, has_r = z > 0, z < nz - 1
+
+    to_sib = {"row": sib, "src": src}
+    to_y = {"row": yp, "src": src}
+    to_x = {"row": row, "src": xp}
+    to_r = {"row": row, "src": src + 2}
+    to_l = {"row": row, "src": src - 2}
+
+    def remote(s, d, ss, rr, dev):
+        return pltpu.make_async_remote_copy(
+            src_ref=s, dst_ref=d, send_sem=ss, recv_sem=rr, device_id=dev, device_id_type=MESH
+        )
+
+    barrier = pltpu.get_barrier_semaphore()
+
+    def hello(dev):
+        pl.semaphore_signal(barrier, inc=1, device_id=dev, device_id_type=MESH)
+
+    for dev in (to_sib, to_y, to_x):
+        hello(dev)
+    pl.when(has_l)(lambda: hello(to_l))
+    pl.when(has_r)(lambda: hello(to_r))
+    pl.semaphore_wait(barrier, 3 + has_l.astype(jnp.int32) + has_r.astype(jnp.int32))
+
+    def right(k, o, own):
+        s = fp.at[k] if own else ga.at[k, o]
+        return remote(s, ga.at[k, o], zr_send.at[k, o], z_recv.at[k, o], to_r)
+
+    def left(k, o, own):
+        s = fp.at[k] if own else ga.at[k, o]
+        return remote(s, ga.at[k, o], zl_send.at[k, o], z_recv.at[k, o], to_l)
+
+    def send_own(k):
+        pl.when(has_r)(lambda: right(k, z, True).start())
+        pl.when(has_l)(lambda: left(k, z, True).start())
+
+    def rows_of(o, par):
+        return pl.ds(pl.multiple_of((2 * o + par) * kc, kc), kc)
+
+    def b_copy(o):
+        return remote(sp.at[rows_of(o, 1 - x)], rb.at[o], b_send.at[o], b_recv.at[o], to_x)
+
+    def passing(k, d):
+        @pl.when(z - d >= 0)
+        def _():
+            right(k, z - d, False).wait_recv()
+            pl.when(has_r)(lambda: right(k, z - d, False).start())
+
+        @pl.when(z + d < nz)
+        def _():
+            left(k, z + d, False).wait_recv()
+            pl.when(has_l)(lambda: left(k, z + d, False).start())
+
+    def c_copy(k):
+        return remote(acc.at[k, 1 - core], rc.at[k], c_send.at[k], c_recv.at[k], to_sib)
+
+    def x_copy(k):
+        return remote(sx.at[k, 1], rx.at[k], x_send.at[k], x_recv.at[k], to_x)
+
+    def y_copy(k):
+        return remote(ty.at[k], ry.at[k], y_send.at[k], y_recv.at[k], to_y)
+
+    send_own(0)
+    for o in range(nz):
+        b_copy(o).start()
+    if nblk > 1:
+        send_own(1)
+    for k in range(nblk):
+        ga[k, z] = fp[k]
+    for o in range(nz):
+        hi, lo = split(sp[rows_of(o, x), :])
+        bh[0, o * kc : (o + 1) * kc] = hi
+        bl[0, o * kc : (o + 1) * kc] = lo
+
+    cols = pl.ds(pl.multiple_of(core * half, half), half)
+    other = pl.ds(pl.multiple_of((1 - core) * half, half), half)
+    solutions = []
+
+    def stage_core(k):
+        c_copy(k).wait_recv()
+        sx[k, 1] = acc[k, core, 1] + rc[k, 1]
+        x_copy(k).start()
+        sx[k, 0] = acc[k, core, 0] + rc[k, 0]
+
+    def stage_x(k):
+        x_copy(k).wait_recv()
+        ty[k] = sx[k, 0] + rx[k]
+        y_copy(k).start()
+        rhs = rs[k * block : (k + 1) * block, cols]
+        for j in range(k):
+            rhs = rhs - dot3(win[k * block : (k + 1) * block, j * block : (j + 1) * block], solutions[j])
+        return rhs
+
+    def stage_y(k, rhs):
+        y_copy(k).wait_recv()
+        solutions.append(dot3(inv[k], rhs - (ty[k] + ry[k])))
+
+    for k in range(nblk):
+        if k > 0 and k + 1 < nblk:
+            send_own(k + 1)
+        rhs = None
+        for d in range(1, max(nz, 4)):
+            if d < nz:
+                passing(k, d)
+            if k > 0:
+                if d == 1:
+                    stage_core(k - 1)
+                elif d == 2:
+                    rhs = stage_x(k - 1)
+                elif d == 3:
+                    stage_y(k - 1, rhs)
+        if k == 0:
+            for o in range(nz):
+                b_copy(o).wait_recv()
+                hi, lo = split(rb[o])
+                bh[1, o * kc : (o + 1) * kc] = hi
+                bl[1, o * kc : (o + 1) * kc] = lo
+        for o in range(nz):
+            hi, lo = split(ga[k, o])
+            ah[:, o * kc : (o + 1) * kc] = hi
+            al[:, o * kc : (o + 1) * kc] = lo
+        for g in range(2):
+            p = dot(ah[...], bh[g]) + (dot(ah[...], bl[g]) + dot(al[...], bh[g]))
+            acc[k, 0, g] = p[:, :half]
+            acc[k, 1, g] = p[:, half:]
+        c_copy(k).start()
+
+    last = nblk - 1
+    stage_core(last)
+    stage_y(last, stage_x(last))
+
+    def pick(r):
+        total = jnp.zeros((block, half), F32)
+        for k in range(nblk):
+            total = total + jnp.where(owner[k] == r, solutions[k], jnp.zeros_like(total))
+        return total
+
+    fs[...] = pick(sib)
+    final = remote(fs, fr, f_sem.at[0], f_sem.at[1], to_sib)
+    final.start()
+    out[:, cols] = pick(row)
+
+    for k in range(nblk):
+        for o in range(nz):
+            pl.when(has_r & (o <= z))(lambda: right(k, o, False).wait_send())
+            pl.when(has_l & (o >= z))(lambda: left(k, o, False).wait_send())
+        c_copy(k).wait_send()
+        x_copy(k).wait_send()
+        y_copy(k).wait_send()
+    for o in range(nz):
+        b_copy(o).wait_send()
+    final.wait()
+    out[:, other] = fr[...]
+
+
+def fast_body(n_row, n_src, front_panel, solved_prev, right_side, front_window, inv_diag, owner_map):
+    nblk, block, kc = front_panel.shape
+    width = solved_prev.shape[1]
+    nz, half = n_src // 2, width // 2
+    vmem = pl.BlockSpec(memory_space=pltpu.VMEM)
+    dma = pltpu.SemaphoreType.DMA
+    return pl.pallas_call(
+        functools.partial(kernel, nz, n_row),
+        out_shape=jax.ShapeDtypeStruct((block, width), F32),
+        in_specs=[pl.BlockSpec(memory_space=pltpu.SMEM)] + [vmem] * 5,
+        out_specs=vmem,
+        scratch_shapes=[
+            pltpu.VMEM((nblk, nz, block, kc), F32),
+            pltpu.VMEM((nz, kc, width), F32),
+            pltpu.VMEM((2, nz * kc, width), BF16),
+            pltpu.VMEM((2, nz * kc, width), BF16),
+            pltpu.VMEM((block, nz * kc), BF16),
+            pltpu.VMEM((block, nz * kc), BF16),
+            pltpu.VMEM((nblk, 2, 2, block, half), F32),
+            pltpu.VMEM((nblk, 2, block, half), F32),
+            pltpu.VMEM((nblk, 2, block, half), F32),
+            pltpu.VMEM((nblk, block, half), F32),
+            pltpu.VMEM((nblk, block, half), F32),
+            pltpu.VMEM((nblk, block, half), F32),
+            pltpu.VMEM((block, half), F32),
+            pltpu.VMEM((block, half), F32),
+            dma((nblk, nz)),
+            dma((nblk, nz)),
+            dma((nblk, nz)),
+            dma((nz,)),
+            dma((nz,)),
+            dma((nblk,)),
+            dma((nblk,)),
+            dma((nblk,)),
+            dma((nblk,)),
+            dma((nblk,)),
+            dma((nblk,)),
+            dma((2,)),
+        ],
+        compiler_params=pltpu.CompilerParams(
+            collective_id=0, has_side_effects=True, vmem_limit_bytes=48 * 2**20
+        ),
+    )(owner_map, front_panel, solved_prev, right_side, front_window, inv_diag)
+
+
 def solution(mesh):
+    n_row, n_src = mesh.shape["row"], mesh.shape["src"]
+
+    def body(front_panel, solved_prev, *rest):
+        nblk, block, kc = front_panel.shape
+        width = solved_prev.shape[1]
+        fits = n_row == 4 and n_src % 2 == 0 and n_src >= 4 and n_src <= 16
+        fits = fits and block % 16 == 0 and kc % 128 == 0 and width % 256 == 0
+        if fits:
+            return fast_body(n_row, n_src, front_panel, solved_prev, *rest)
+        return general_body(front_panel, solved_prev, *rest)
+
     in_specs = (P(None, None, ("row", "src")), P("row", "src"), P(None, "src"), P(), P(), P())
     out_specs = P("row", "src")
     return jax.shard_map(body, mesh=mesh, in_specs=in_specs, out_specs=out_specs, check_vma=False)

time: 169 us -> 81.2 us (0.48)
  waiting for transfers between devices: 136 us -> 0 us
  Pallas kernels: 0 us -> 74.4 us
  matrix products: 16.1 us -> 0 us
  between operations: 15.4 us -> 0.01 us
  local copies, waits for them, and re-layouts: 0.92 us -> 6.35 us
    all_gather x1 -> x0, waiting for transfers between devices: 105 us -> none  [body(): panel_rows = lax.all_gather(front_panel, 'src', axis=2, tiled=True)]
    pallas_call x0 -> x1, Pallas kernels: none -> 74.4 us  [fast_body(): pl.pallas_call(functools.partial(kernel, nz, n_row), out_shape=jax.ShapeD...]
    psum x1 -> x0, waiting for transfers between devices: 30.4 us -> none  [body(): partials = lax.psum(local, 'row')]
    dot_general x6 -> x0, matrix products: 16.1 us -> none  [the longest x1 8.01 us: body(): jnp.einsum('kbn,ns->kbs', panel_rows, solved_prev, precision=highest, pre...]
    unnamed x6 -> x11, local copies, waits for them, and re-layouts: 0.01 us -> 6.35 us
  transfers between devices with their start and end apart: 2 -> 0, of which waited for: 2 -> 0; matrix products, arithmetic and copies ran while one was open for 0% -> 0% of each run, Pallas kernels for 0% -> 0%
where the time goes in v1:
time: 81.2 us; the launch traced here: 80.8 us
  Pallas kernels  74.4 us (92%)
  local copies, waits for them, and re-layouts  6.35 us (8%)
    pallas_call x1, Pallas kernels, fast_body(): pl.pallas_call(functools.partial(kernel, nz, n_row), out_shape=jax.ShapeD...  74.4 us
    unnamed x11, local copies, waits for them, and re-layouts  6.35 us

profile of v1, /device:TPU:0, one launch (start us, length us, event | category | flops | bytes accessed | tf_op | source)
XLA Modules:
  0.0 80.8 jit_solution(6864853199727933393)
XLA Ops:
  0.0 0.0 copy-start
  0.0 1.6 %copy-done = f32[2048,256]{1,0:T(8,128)S(1)} copy-done((f32[2048,256]{1,0:T(8,128)S(1)}, f32[2048,256]{1,0:T(8,128)}, u32[]{:S(2)}) %copy-start) | copy-done | bytes 2097176
  1.6 0.0 copy-start.1
  1.6 1.1 %copy-done.1 = f32[3,256,256]{2,1,0:T(8,128)S(1)} copy-done((f32[3,256,256]{2,1,0:T(8,128)S(1)}, f32[3,256,256]{2,1,0:T(8,128)}, u32[]{:S(2)}) %copy-start.1) | copy-done | bytes 786456
  2.7 0.0 copy-start.2
  2.7 1.1 %copy-done.2 = f32[768,256]{1,0:T(8,128)S(1)} copy-done((f32[768,256]{1,0:T(8,128)S(1)}, f32[768,256]{1,0:T(8,128)}, u32[]{:S(2)}) %copy-start.2) | copy-done | bytes 786456
  3.9 0.0 copy-start.3
  3.9 1.1 %copy-done.3 = f32[3,256,256]{2,1,0:T(8,128)S(1)} copy-done((f32[3,256,256]{2,1,0:T(8,128)S(1)}, f32[3,256,256]{2,1,0:T(8,128)}, u32[]{:S(2)}) %copy-start.3) | copy-done | bytes 786456
  5.0 0.0 copy-start.4
  5.0 0.7 copy-done.4
  5.6 74.4 %shard_map.64 = f32[256,256]{1,0:T(8,128)S(1)} custom-call(s32[3]{0:T(128)S(1)} %copy-done.4, f32[3,256,256]{2,1,0:T(8,128)S(1)} %copy-done.1, f32[2048,256]{1,0:T(8,128)S(1)} %copy-done, f32[768,256]{1,0:T(8,128)S(1)} %copy-done.2, f32[768,768]{1,0:T(8,128)} %win.1, f32[3,256,256]{2,1,0:T(8,128)S(1)} %copy-done.3), custom_call_target="tpu_custom_call" | custom-call | tf_op jit(solution)/shard_map/pallas_call | solution.py:238
  80.1 0.7 copy.8
Async XLA Ops:
  0.0 1.6 %copy-start = (f32[2048,256]{1,0:T(8,128)S(1)}, f32[2048,256]{1,0:T(8,128)}, u32[]{:S(2)}) copy-start(f32[2048,256]{1,0:T(8,128)} %sp.1) | copy-start | bytes 6291460
  1.6 1.1 %copy-start.1 = (f32[3,256,256]{2,1,0:T(8,128)S(1)}, f32[3,256,256]{2,1,0:T(8,128)}, u32[]{:S(2)}) copy-start(f32[3,256,256]{2,1,0:T(8,128)} %fp.1) | copy-start | bytes 2359300
  2.7 1.1 %copy-start.2 = (f32[768,256]{1,0:T(8,128)S(1)}, f32[768,256]{1,0:T(8,128)}, u32[]{:S(2)}) copy-start(f32[768,256]{1,0:T(8,128)} %rs.1) | copy-start | bytes 2359300
  3.9 1.1 %copy-start.3 = (f32[3,256,256]{2,1,0:T(8,128)S(1)}, f32[3,256,256]{2,1,0:T(8,128)}, u32[]{:S(2)}) copy-start(f32[3,256,256]{2,1,0:T(8,128)} %inv.1) | copy-start | bytes 2359300
  5.0 0.7 copy-start.4

commit v2 on v0

--- a/solution.py
+++ b/solution.py
@@ -1,10 +1,18 @@
+import functools
+
 import jax
 import jax.numpy as jnp
 from jax import lax
+from jax.experimental import pallas as pl
+from jax.experimental.pallas import tpu as pltpu
 from jax.sharding import PartitionSpec as P
 
-
-def body(front_panel, solved_prev, right_side, front_window, inv_diag, owner_map):
+F32 = jnp.float32
+BF16 = jnp.bfloat16
+MESH = pl.DeviceIdType.MESH
+
+
+def general_body(front_panel, solved_prev, right_side, front_window, inv_diag, owner_map):
     highest = lax.Precision.HIGHEST
     nblk = front_panel.shape[0]
     block = front_panel.shape[1]
@@ -22,8 +30,7 @@
     stored = jnp.zeros((block, width), jnp.float32)
     solutions = []
     for k in range(nblk):
-        partial_value = partials[k]
-        rhs = right_side[k * block : (k + 1) * block] - partial_value
+        rhs = right_side[k * block : (k + 1) * block] - partials[k]
         if k > 0:
             earlier = jnp.concatenate(solutions, axis=0)
             rhs = rhs - jnp.dot(
@@ -39,7 +46,307 @@
     return stored
 
 
+def split(v):
+    hi = v.astype(BF16)
+    return hi, (v - hi.astype(F32)).astype(BF16)
+
+
+def dot(a, b):
+    return jnp.dot(a, b, preferred_element_type=F32)
+
+
+def dot3(a, b):
+    (ah, al), (bh, bl) = split(a), split(b)
+    return dot(ah, bh) + (dot(ah, bl) + dot(al, bh))
+
+
+def kernel(
+    nz, n_row, cut, owner, fp, sp, rs_hbm, win_hbm, inv_hbm, out,
+    ga, rb, sv, rs, win, inv, bh, bl, acc, rc, sx, rx, ty, ry, fs, fr,
+    zr_send, zl_send, z_recv, b_send, b_recv, c_send, c_recv, x_send, x_recv, y_send, y_recv, f_sem, l_sem, g_sem, s_sem,
+):
+    pieces, rows, kc = fp.shape
+    width = sp.shape[1]
+    half = width // 2
+    nblk = pieces // cut
+    block = rows * cut
+    row, src = lax.axis_index("row"), lax.axis_index("src")
+    z, x = src // 2, lax.rem(src, 2)
+    core = lax.rem(row, 2)
+    sib = row + 1 - 2 * core
+    yp = lax.rem(row + 2, n_row)
+    xp = src + 1 - 2 * x
+    has_l, has_r = z > 0, z < nz - 1
+
+    to_sib = {"row": sib, "src": src}
+    to_y = {"row": yp, "src": src}
+    to_x = {"row": row, "src": xp}
+    to_r = {"row": row, "src": src + 2}
+    to_l = {"row": row, "src": src - 2}
+
+    def remote(s, d, ss, rr, dev):
+        return pltpu.make_async_remote_copy(
+            src_ref=s, dst_ref=d, send_sem=ss, recv_sem=rr, device_id=dev, device_id_type=MESH
+        )
+
+    def rows_of(o, par):
+        return pl.ds(pl.multiple_of((2 * o + par) * kc, kc), kc)
+
+    def own_copy(p):
+        return pltpu.make_async_copy(fp.at[p], ga.at[p, z], g_sem.at[p])
+
+    def sv_copy(o):
+        return pltpu.make_async_copy(sp.at[rows_of(o, x)], sv.at[o], s_sem.at[o])
+
+    small = [
+        pltpu.make_async_copy(rs_hbm, rs, l_sem.at[0]),
+        pltpu.make_async_copy(win_hbm, win, l_sem.at[1]),
+        pltpu.make_async_copy(inv_hbm, inv, l_sem.at[2]),
+    ]
+
+    barrier = pltpu.get_barrier_semaphore()
+
+    def hello(dev):
+        pl.semaphore_signal(barrier, inc=1, device_id=dev, device_id_type=MESH)
+
+    for dev in (to_sib, to_y, to_x):
+        hello(dev)
+    pl.when(has_l)(lambda: hello(to_l))
+    pl.when(has_r)(lambda: hello(to_r))
+    for o in range(nz):
+        sv_copy(o).start()
+    for p in range(pieces):
+        own_copy(p).start()
+    for copy in small:
+        copy.start()
+    pl.semaphore_wait(barrier, 3 + has_l.astype(jnp.int32) + has_r.astype(jnp.int32))
+
+    def right(p, o, own=False):
+        s = fp.at[p] if own else ga.at[p, o]
+        return remote(s, ga.at[p, o], zr_send.at[p, o], z_recv.at[p, o], to_r)
+
+    def left(p, o, own=False):
+        s = fp.at[p] if own else ga.at[p, o]
+        return remote(s, ga.at[p, o], zl_send.at[p, o], z_recv.at[p, o], to_l)
+
+    def b_copy(o):
+        return remote(sp.at[rows_of(o, 1 - x)], rb.at[o], b_send.at[o], b_recv.at[o], to_x)
+
+    def passing(p, d):
+        @pl.when(z - d >= 0)
+        def _():
+            right(p, z - d).wait_recv()
+            pl.when(has_r)(lambda: right(p, z - d).start())
+
+        @pl.when(z + d < nz)
+        def _():
+            left(p, z + d).wait_recv()
+            pl.when(has_l)(lambda: left(p, z + d).start())
+
+    def each(body):
+        lax.fori_loop(0, pieces, lambda p, c: (body(p), c)[1], 0)
+
+    for p in range(pieces):
+        pl.when(has_r)(lambda p=p: right(p, z, True).start())
+        pl.when(has_l)(lambda p=p: left(p, z, True).start())
+        if p < nz:
+            b_copy(p).start()
+    for o in range(pieces, nz):
+        b_copy(o).start()
+
+    for o in range(nz):
+        sv_copy(o).wait()
+        hi, lo = split(sv[o])
+        bh[0, o * kc : (o + 1) * kc] = hi
+        bl[0, o * kc : (o + 1) * kc] = lo
+
+    each(lambda p: passing(p, 1))
+    for copy in small:
+        copy.wait()
+    for o in range(nz):
+        b_copy(o).wait_recv()
+        hi, lo = split(rb[o])
+        bh[1, o * kc : (o + 1) * kc] = hi
+        bl[1, o * kc : (o + 1) * kc] = lo
+
+    def product(p, o, first=False):
+        hi, lo = split(ga[p, o])
+        at = pl.ds(pl.multiple_of(o * kc, kc), kc)
+        for g in range(2):
+            t = dot(hi, bh[g, at]) + (dot(hi, bl[g, at]) + dot(lo, bh[g, at]))
+            if first:
+                acc[p, 0, g] = t[:, :half]
+                acc[p, 1, g] = t[:, half:]
+            else:
+                acc[p, 0, g] += t[:, :half]
+                acc[p, 1, g] += t[:, half:]
+
+    def own_product(p):
+        own_copy(p).wait()
+        product(p, z, True)
+
+    def products(p, d):
+        if 2 * d >= nz:
+            some = (z - d >= 0) | (z + d < nz)
+            pl.when(some)(lambda: product(p, jnp.where(z - d >= 0, z - d, z + d)))
+        else:
+            pl.when(z - d >= 0)(lambda: product(p, z - d))
+            pl.when(z + d < nz)(lambda: product(p, z + d))
+
+    each(own_product)
+    each(lambda p: products(p, 1))
+    for d in range(2, nz - 1):
+
+        def both(p, d=d):
+            passing(p, d)
+            products(p, d)
+
+        each(both)
+
+    def c_copy(p):
+        return remote(acc.at[p, 1 - core], rc.at[p], c_send.at[p], c_recv.at[p], to_sib)
+
+    def x_copy(p):
+        return remote(sx.at[p, 1], rx.at[p], x_send.at[p], x_recv.at[p], to_x)
+
+    def y_copy(p):
+        return remote(ty.at[p], ry.at[p], y_send.at[p], y_recv.at[p], to_y)
+
+    cols = pl.ds(pl.multiple_of(core * half, half), half)
+    other = pl.ds(pl.multiple_of((1 - core) * half, half), half)
+    solutions = []
+    rhs = [None]
+
+    def stage_core(p):
+        c_copy(p).wait_recv()
+        sx[p, 1] = acc[p, core, 1] + rc[p, 1]
+        x_copy(p).start()
+        sx[p, 0] = acc[p, core, 0] + rc[p, 0]
+
+    def stage_x(p):
+        x_copy(p).wait_recv()
+        ty[p] = sx[p, 0] + rx[p]
+        y_copy(p).start()
+
+    def prepare(k):
+        v = rs[k * block : (k + 1) * block, cols]
+        for j in range(k):
+            v = v - dot3(win[k * block : (k + 1) * block, j * block : (j + 1) * block], solutions[j])
+        return v
+
+    def stage_y(p):
+        y_copy(p).wait_recv()
+        if p % cut == cut - 1:
+            k = p // cut
+            total = jnp.concatenate([ty[q] + ry[q] for q in range(k * cut, p + 1)], axis=0)
+            solutions.append(dot3(inv[k], (rhs[0] if rhs[0] is not None else prepare(k)) - total))
+            rhs[0] = prepare(k + 1) if k + 1 < nblk else None
+
+    for step in range(pieces + 3):
+        if step < pieces:
+            if nz > 2:
+                passing(step, nz - 1)
+                products(step, nz - 1)
+            c_copy(step).start()
+        if 0 <= step - 1 < pieces:
+            stage_core(step - 1)
+        if 0 <= step - 2 < pieces:
+            stage_x(step - 2)
+        if 0 <= step - 3 < pieces:
+            stage_y(step - 3)
+
+    def pick(r):
+        total = jnp.zeros((block, half), F32)
+        for k in range(nblk):
+            total = total + jnp.where(owner[k] == r, solutions[k], jnp.zeros_like(total))
+        return total
+
+    fs[...] = pick(sib)
+    final = remote(fs, fr, f_sem.at[0], f_sem.at[1], to_sib)
+    final.start()
+    out[:, cols] = pick(row)
+
+    def settle(p):
+        for o in range(nz):
+            pl.when(has_r & (o <= z))(lambda o=o: right(p, o).wait_send())
+            pl.when(has_l & (o >= z))(lambda o=o: left(p, o).wait_send())
+        c_copy(p).wait_send()
+        x_copy(p).wait_send()
+        y_copy(p).wait_send()
+
+    each(settle)
+    for o in range(nz):
+        b_copy(o).wait_send()
+    final.wait()
+    out[:, other] = fr[...]
+
+
+def fast_body(n_row, n_src, front_panel, solved_prev, right_side, front_window, inv_diag, owner_map):
+    nblk, block, kc = front_panel.shape
+    width = solved_prev.shape[1]
+    nz, half = n_src // 2, width // 2
+    cut = 2
+    pieces, rows = nblk * cut, block // cut
+    hbm = pl.BlockSpec(memory_space=pl.ANY)
+    dma = pltpu.SemaphoreType.DMA
+    return pl.pallas_call(
+        functools.partial(kernel, nz, n_row, cut),
+        out_shape=jax.ShapeDtypeStruct((block, width), F32),
+        in_specs=[pl.BlockSpec(memory_space=pltpu.SMEM)] + [hbm] * 5,
+        out_specs=pl.BlockSpec(memory_space=pltpu.VMEM),
+        scratch_shapes=[
+            pltpu.VMEM((pieces, nz, rows, kc), F32),
+            pltpu.VMEM((nz, kc, width), F32),
+            pltpu.VMEM((nz, kc, width), F32),
+            pltpu.VMEM(right_side.shape, F32),
+            pltpu.VMEM(front_window.shape, F32),
+            pltpu.VMEM(inv_diag.shape, F32),
+            pltpu.VMEM((2, nz * kc, width), BF16),
+            pltpu.VMEM((2, nz * kc, width), BF16),
+            pltpu.VMEM((pieces, 2, 2, rows, half), F32),
+            pltpu.VMEM((pieces, 2, rows, half), F32),
+            pltpu.VMEM((pieces, 2, rows, half), F32),
+            pltpu.VMEM((pieces, rows, half), F32),
+            pltpu.VMEM((pieces, rows, half), F32),
+            pltpu.VMEM((pieces, rows, half), F32),
+            pltpu.VMEM((block, half), F32),
+            pltpu.VMEM((block, half), F32),
+            dma((pieces, nz)),
+            dma((pieces, nz)),
+            dma((pieces, nz)),
+            dma((nz,)),
+            dma((nz,)),
+            dma((pieces,)),
+            dma((pieces,)),
+            dma((pieces,)),
+            dma((pieces,)),
+            dma((pieces,)),
+            dma((pieces,)),
+            dma((2,)),
+            dma((3,)),
+            dma((pieces,)),
+            dma((nz,)),
+        ],
+        compiler_params=pltpu.CompilerParams(
+            collective_id=0, has_side_effects=True, vmem_limit_bytes=56 * 2**20
+        ),
+    )(
+        owner_map, front_panel.reshape(pieces, rows, kc), solved_prev, right_side, front_window, inv_diag
+    )
+
+
 def solution(mesh):
+    n_row, n_src = mesh.shape["row"], mesh.shape["src"]
+
+    def body(front_panel, solved_prev, *rest):
+        nblk, block, kc = front_panel.shape
+        width = solved_prev.shape[1]
+        fits = n_row == 4 and n_src % 2 == 0 and n_src >= 4 and n_src <= 16
+        fits = fits and block % 32 == 0 and kc % 128 == 0 and width % 256 == 0
+        if fits:
+            return fast_body(n_row, n_src, front_panel, solved_prev, *rest)
+        return general_body(front_panel, solved_prev, *rest)
+
     in_specs = (P(None, None, ("row", "src")), P("row", "src"), P(None, "src"), P(), P(), P())
     out_specs = P("row", "src")
     return jax.shard_map(body, mesh=mesh, in_specs=in_specs, out_specs=out_specs, check_vma=False)

time: 169 us -> 71.5 us (0.42)
  waiting for transfers between devices: 136 us -> 0 us
  Pallas kernels: 0 us -> 69.7 us
  matrix products: 16.1 us -> 0 us
  between operations: 15.4 us -> 0.01 us
    all_gather x1 -> x0, waiting for transfers between devices: 105 us -> none  [body(): panel_rows = lax.all_gather(front_panel, 'src', axis=2, tiled=True)]
    pallas_call x0 -> x1, Pallas kernels: none -> 69.7 us  [fast_body(): pl.pallas_call(functools.partial(kernel, nz, n_row, cut), out_shape=jax.S...]
    psum x1 -> x0, waiting for transfers between devices: 30.4 us -> none  [body(): partials = lax.psum(local, 'row')]
    dot_general x6 -> x0, matrix products: 16.1 us -> none  [the longest x1 8.01 us: body(): jnp.einsum('kbn,ns->kbs', panel_rows, solved_prev, precision=highest, pre...]
  transfers between devices with their start and end apart: 2 -> 0, of which waited for: 2 -> 0; matrix products, arithmetic and copies ran while one was open for 0% -> 0% of each run, Pallas kernels for 0% -> 0%
where the time goes in v2:
time: 71.5 us; the launch traced here: 71.4 us
  Pallas kernels  69.7 us (97%)
  local copies, waits for them, and re-layouts  1.67 us (2%)
    pallas_call x1, Pallas kernels, fast_body(): pl.pallas_call(functools.partial(kernel, nz, n_row, cut), out_shape=jax.S...  69.7 us
    unnamed x1, local copies, waits for them, and re-layouts  1.67 us

profile of v2, /device:TPU:0, one launch (start us, length us, event | category | flops | bytes accessed | tf_op | source)
XLA Modules:
  0.0 71.4 jit_solution(14479946922742419786)
XLA Ops:
  0.0 69.7 %shard_map.64 = f32[256,256]{1,0:T(8,128)} custom-call(s32[3]{0:T(128)} %owner.1, f32[6,128,256]{2,1,0:T(8,128)} %bitcast.1, f32[2048,256]{1,0:T(8,128)} %sp.1, f32[768,256]{1,0:T(8,128)} %rs_hbm.1, f32[768,768]{1,0:T(8,128)} %win_hbm.1, f32[3,256,256]{2,1,0:T(8,128)} %inv_hbm.1), custom_call_target="tpu_custom_call" | custom-call | tf_op jit(solution)/shard_map/pallas_call | solution.py:292
  69.7 1.7 %copy.8 = f32[256,256]{1,0:T(8,128)} copy(f32[256,256]{1,0:T(8,128)} %shard_map.64) | data formatting | bytes 524288

commit v3 on v2

--- a/solution.py
+++ b/solution.py
@@ -242,18 +242,17 @@
             solutions.append(dot3(inv[k], (rhs[0] if rhs[0] is not None else prepare(k)) - total))
             rhs[0] = prepare(k + 1) if k + 1 < nblk else None
 
-    for step in range(pieces + 3):
+    for step in range(pieces + 2):
         if step < pieces:
             if nz > 2:
                 passing(step, nz - 1)
                 products(step, nz - 1)
             c_copy(step).start()
+            stage_core(step)
         if 0 <= step - 1 < pieces:
-            stage_core(step - 1)
+            stage_x(step - 1)
         if 0 <= step - 2 < pieces:
-            stage_x(step - 2)
-        if 0 <= step - 3 < pieces:
-            stage_y(step - 3)
+            stage_y(step - 2)
 
     def pick(r):
         total = jnp.zeros((block, half), F32)

time: 71.5 us -> 70.7 us (0.989)
  Pallas kernels: 69.7 us -> 68.8 us
    pallas_call x1, Pallas kernels: 69.7 us -> 68.8 us  [fast_body(): pl.pallas_call(functools.partial(kernel, nz, n_row, cut), out_shape=jax.S...]
where the time goes in v3:
time: 70.7 us; the launch traced here: 70.5 us
  Pallas kernels  68.8 us (97%)
  local copies, waits for them, and re-layouts  1.67 us (2%)
    pallas_call x1, Pallas kernels, fast_body(): pl.pallas_call(functools.partial(kernel, nz, n_row, cut), out_shape=jax.S...  68.8 us
    unnamed x1, local copies, waits for them, and re-layouts  1.67 us

profile of v3, /device:TPU:0, one launch (start us, length us, event | category | flops | bytes accessed | tf_op | source)
XLA Modules:
  0.0 70.5 jit_solution(8848609415796870670)
XLA Ops:
  0.0 68.8 %shard_map.64 = f32[256,256]{1,0:T(8,128)} custom-call(s32[3]{0:T(128)} %owner.1, f32[6,128,256]{2,1,0:T(8,128)} %bitcast.1, f32[2048,256]{1,0:T(8,128)} %sp.1, f32[768,256]{1,0:T(8,128)} %rs_hbm.1, f32[768,768]{1,0:T(8,128)} %win_hbm.1, f32[3,256,256]{2,1,0:T(8,128)} %inv_hbm.1), custom_call_target="tpu_custom_call" | custom-call | tf_op jit(solution)/shard_map/pallas_call | solution.py:291
  68.8 1.7 %copy.8 = f32[256,256]{1,0:T(8,128)} copy(f32[256,256]{1,0:T(8,128)} %shard_map.64) | data formatting | bytes 524288
